TPU v7x, 32 devices: a whole 2x2x4 slice. The times are simulated.
32 devices in a mesh: xy: 16 (over z, x, core), gz: 2 (over y).
Axes of the slice: x: 2, y: 2, z: 4, core: 2. Of those that a mesh axis runs over, the one named last changes fastest.
Arguments:
- conductivity: float32 [32, 256, 512], P('gz', 'xy'), may hold values from 0.5 to 2
- start_fields: float32 [4, 32, 256, 512], P(None, 'gz', 'xy'), may hold values from -6 to 6
- electrodes: int32 [3, 4, 64], replicated, may hold values from 0 to 511, as said below
- currents: float32 [4, 64], replicated, may hold values from -16 to 16
- pair_table: int32 [4, 2], replicated, may hold values from 0 to 1
- bounds: float32 [2], replicated, may hold values from 0.05 to 30, as said below
Outputs:
- potentials: float32 [4, 32, 256, 512], P(None, 'gz', 'xy')
- sensitivity: float32 [4, 32, 256, 512], P(None, 'gz', 'xy')
Inputs may be any that keep to these rules, and one draw needn't show every extreme that they name: `electrodes`: each index lies inside the grid along its own dimension. `bounds`: the first entry is positive and the second exceeds the largest eigenvalue of A.
All inputs are finite; a program needn't handle non-finite values.
Results may differ from a plain program's by a relative error of at most 0.00021.
Values sent between devices are 32-bit elements; how exact they have to be, the bound alone decides.
A program may use at most 128 MiB of HBM per device.

v0:
```python
import functools
import math

import jax
import jax.numpy as jnp
import ml_dtypes
import numpy as np
from jax import lax
from jax.experimental import pallas as pl
from jax.experimental.pallas import tpu as pltpu
from jax.sharding import PartitionSpec as P

DEGREE = 4
SWEEPS = 2
REACH = 4
MESH = pl.DeviceIdType.MESH
F32 = jnp.float32
BF16 = jnp.bfloat16


def prior_taps():
    raw = [
        (1.0 + math.sqrt(3.0) * k / 2.0) * math.exp(-math.sqrt(3.0) * k / 2.0)
        for k in range(REACH + 1)
    ]
    total = raw[0] + 2.0 * sum(raw[1:])
    return [v / total for v in raw]


def split_taps():
    taps = np.asarray(prior_taps(), np.float32)
    high = taps.astype(ml_dtypes.bfloat16).astype(np.float32)
    return [float(v) for v in high], [float(v) for v in taps - high]


def band(distance, inside=None):
    parts = []
    for taps in split_taps():
        out = jnp.zeros(distance.shape, F32)
        for k in range(REACH + 1):
            hit = jnp.abs(distance) == k
            if inside is not None:
                hit = hit & inside
            out = jnp.where(hit, taps[k], out)
        parts.append(out.astype(BF16))
    return parts


def halves(a):
    high = a.astype(BF16)
    return high, (a - high.astype(F32)).astype(BF16)


def dot(a, b):
    return lax.dot_general(a, b, (((1,), (0,)), ((), ())), preferred_element_type=F32)


def kernel(
    pair_ref, bounds_ref, elec_ref, cur_ref, cond_hbm, start_hbm, pot_hbm, sens_hbm,
    cp, v, x, r, rowx, sfx, rcx, scx, cz, cxm, cxp, cym, cyp, cd, raw, u, w, xs, xr, sens, coef,
    ty, tc, te,
    load_sem, out_sem, send_sem, recv_sem, csend, crecv, zsend, zrecv, xsend, xrecv,
):
    fields, nz, nx, ny = x.shape
    pairs = u.shape[0]
    cells = nz * nx
    ix, iz = lax.axis_index("xy"), lax.axis_index("gz")
    has = [ix > 0, ix < lax.axis_size("xy") - 1, iz > 0, iz < lax.axis_size("gz") - 1]
    place = [
        (ix - 1, iz), (ix + 1, iz), (ix, iz - 1), (ix, iz + 1),
    ]

    barrier = pltpu.get_barrier_semaphore()
    loads = [pltpu.make_async_copy(cond_hbm, cp.at[pl.ds(1, nz)], load_sem.at[0])]
    for f in range(fields):
        loads.append(
            pltpu.make_async_copy(start_hbm.at[f], v.at[0, f, pl.ds(1, nz)], load_sem.at[1 + f])
        )
    loads.append(pltpu.make_async_copy(start_hbm, x, load_sem.at[1 + fields]))
    for copy in loads:
        copy.start()

    for d in range(4):
        @pl.when(jnp.logical_not(has[d]))
        def _():
            if d < 2:
                rcx[d] = jnp.zeros(rcx.shape[1:], F32)
                for slot in range(2):
                    for f in range(fields):
                        rowx[slot, f, d] = jnp.zeros(rowx.shape[3:], F32)
                for p in range(pairs):
                    xr[p, d] = jnp.zeros(xr.shape[2:], F32)
            else:
                edge = 0 if d == 2 else nz + 1
                cp[edge] = jnp.zeros((nx, ny), F32)
                for slot in range(2):
                    for f in range(fields):
                        v[slot, f, edge] = jnp.zeros((nx, ny), F32)
                first = 0 if d == 2 else nz + REACH
                for p in range(pairs):
                    u[p, first:first + REACH] = jnp.zeros((REACH, nx, ny), F32)

    for d in range(4):
        @pl.when(has[d])
        def _():
            pl.semaphore_signal(barrier, inc=1, device_id=place[d], device_id_type=MESH)
    pl.semaphore_wait(barrier, sum(h.astype(jnp.int32) for h in has))

    def field_copy(slot, f, d):
        o = d ^ 1
        if d < 2:
            src, dst = sfx.at[f, d], rowx.at[slot, f, o]
        else:
            src = v.at[slot, f, 1 if d == 2 else nz]
            dst = v.at[slot, f, nz + 1 if d == 2 else 0]
        return pltpu.make_async_remote_copy(
            src_ref=src, dst_ref=dst, send_sem=send_sem.at[f, d],
            recv_sem=recv_sem.at[slot, f, o], device_id=place[d], device_id_type=MESH,
        )

    def field_arrival(slot, f, d):
        if d < 2:
            src, dst = sfx.at[f, d], rowx.at[slot, f, d]
        else:
            src = v.at[slot, f, 1 if d == 2 else nz]
            dst = v.at[slot, f, 0 if d == 2 else nz + 1]
        return pltpu.make_async_remote_copy(
            src_ref=src, dst_ref=dst, send_sem=send_sem.at[f, d],
            recv_sem=recv_sem.at[slot, f, d], device_id=place[d], device_id_type=MESH,
        )

    def cond_copy(d, arrives):
        o = d if arrives else d ^ 1
        if d < 2:
            src, dst = scx.at[d], rcx.at[o]
        else:
            src = cp.at[1 if d == 2 else nz]
            dst = cp.at[0 if o == 2 else nz + 1]
        return pltpu.make_async_remote_copy(
            src_ref=src, dst_ref=dst, send_sem=csend.at[d], recv_sem=crecv.at[o],
            device_id=place[d], device_id_type=MESH,
        )

    def send_field(slot, f):
        for d in range(4):
            @pl.when(has[d])
            def _():
                field_copy(slot, f, d).start()

    def wait_field(slot, f):
        for d in range(4):
            @pl.when(has[d])
            def _():
                field_arrival(slot, f, d).wait_recv()
                field_copy(slot, f, d).wait_send()

    loads[0].wait()

    @pl.loop(0, nz)
    def _(z):
        scx[0, z] = cp[z + 1, 0:1, :]
        scx[1, z] = cp[z + 1, nx - 1:nx, :]

    for d in range(4):
        @pl.when(has[d])
        def _():
            cond_copy(d, False).start()
    for f in range(fields):
        loads[1 + f].wait()

        @pl.loop(0, nz)
        def _(z):
            sfx[f, 0, z] = v[0, f, z + 1, 0:1, :]
            sfx[f, 1, z] = v[0, f, z + 1, nx - 1:nx, :]

        send_field(0, f)

    low = jnp.full((1, ny), bounds_ref[0], F32)
    high = jnp.full((1, ny), bounds_ref[1], F32)
    theta = 0.5 * (low + high)
    delta = 0.5 * (high - low)
    ratio = theta / delta
    for sweep in range(SWEEPS):
        rho = 1.0 / ratio
        for k in range(DEGREE):
            j = sweep * DEGREE + k
            if k == 0:
                coef[j, 0] = jnp.zeros((1, ny), F32)
                coef[j, 1] = 1.0 / theta
            else:
                rho_new = 1.0 / (2.0 * ratio - rho)
                coef[j, 0] = rho_new * rho
                coef[j, 1] = 2.0 * rho_new / delta
                rho = rho_new

    count = cur_ref.shape[1]
    cell_ids = lax.broadcasted_iota(jnp.int32, (cells, count), 0)
    second_ids = lax.broadcasted_iota(jnp.int32, (ny, count), 0)
    for f in range(fields):
        lz = elec_ref[0, f:f + 1, :] - iz * nz
        lx = elec_ref[1, f:f + 1, :] - ix * nx
        inside = (lz >= 0) & (lz < nz) & (lx >= 0) & (lx < nx)
        code = jnp.where(inside, lz * nx + lx, -1)
        at_cell = cell_ids == code
        at_second = jnp.where(second_ids == elec_ref[2, f:f + 1, :], 1.0, 0.0).astype(BF16)
        rest = cur_ref[f:f + 1, :]
        terms = []
        for _ in range(3):
            part = rest.astype(BF16).astype(F32)
            rest = rest - part
            left = jnp.where(at_cell, part, 0.0).astype(BF16)
            terms.append(
                lax.dot_general(
                    left, at_second, (((1,), (1,)), ((), ())), preferred_element_type=F32
                )
            )
        r[f] = ((terms[2] + terms[1]) + terms[0]).reshape(nz, nx, ny)

    a = lax.broadcasted_iota(jnp.int32, (ny, ny), 0)
    b = lax.broadcasted_iota(jnp.int32, (ny, ny), 1)
    ty[0], ty[1] = band(a - b)
    a = lax.broadcasted_iota(jnp.int32, (cells, cells), 0)
    b = lax.broadcasted_iota(jnp.int32, (cells, cells), 1)
    tc[0], tc[1] = band(a % nx - b % nx, a // nx == b // nx)
    rim = nz * REACH
    a = lax.broadcasted_iota(jnp.int32, (cells, rim), 0)
    b = lax.broadcasted_iota(jnp.int32, (cells, rim), 1)
    same = a // nx == b // REACH
    te[0, 0], te[0, 1] = band(a % nx - (b % REACH - REACH), same)
    te[1, 0], te[1, 1] = band(a % nx - (b % REACH + nx), same)

    rows = lax.broadcasted_iota(jnp.int32, (nx, ny), 0)
    lanes = lax.broadcasted_iota(jnp.int32, (nx, ny), 1)

    def x_down(a, row):
        return jnp.where(rows == 0, row, pltpu.roll(a, 1, 0))

    def x_up(a, row):
        return jnp.where(rows == nx - 1, row, pltpu.roll(a, nx - 1, 0))

    for d in range(4):
        @pl.when(has[d])
        def _():
            cond_copy(d, True).wait_recv()
            cond_copy(d, False).wait_send()

    @pl.loop(0, nz)
    def _(z):
        c = cp[z + 1]
        half = 0.5 * c
        zm = half + 0.5 * cp[z]
        zp = half + 0.5 * cp[z + 2]
        xm = half + 0.5 * x_down(c, rcx[0, z])
        xp = half + 0.5 * x_up(c, rcx[1, z])
        ym = half + 0.5 * jnp.where(lanes == 0, 0.0, pltpu.roll(c, 1, 1))
        yp = half + 0.5 * jnp.where(lanes == ny - 1, 0.0, pltpu.roll(c, ny - 1, 1))
        cz[z] = zm
        cz[z + 1] = zp
        cxm[z] = xm
        cxp[z] = xp
        cym[z] = jnp.where(lanes == 0, 0.0, ym)
        cyp[z] = jnp.where(lanes == ny - 1, 0.0, yp)
        cd[z] = ((zm + zp) + (xm + xp)) + (ym + yp)

    loads[1 + fields].wait()

    def step(j, last):
        slot = lax.rem(j, 2)
        later = 1 - slot
        fac_d = coef[j, 0]
        fac_r = coef[j, 1]
        for f in range(fields):
            wait_field(slot, f)

            @pl.loop(0, nz, unroll=2)
            def _(z):
                c = v[slot, f, z + 1]
                total = cz[z] * v[slot, f, z] + cz[z + 1] * v[slot, f, z + 2]
                total = total + cxm[z] * x_down(c, rowx[slot, f, 0, z])
                total = total + cxp[z] * x_up(c, rowx[slot, f, 1, z])
                total = total + cym[z] * pltpu.roll(c, 1, 1)
                total = total + cyp[z] * pltpu.roll(c, ny - 1, 1)
                res = r[f, z] + (total - cd[z] * c)
                new = fac_d * c + fac_r * res
                at = x[f, z] + new
                if last:
                    new = at
                else:
                    r[f, z] = res
                    x[f, z] = at
                v[later, f, z + 1] = new
                sfx[f, 0, z] = new[0:1, :]
                sfx[f, 1, z] = new[nx - 1:nx, :]

            send_field(later, f)
            if last:
                pltpu.make_async_copy(
                    v.at[later, f, pl.ds(1, nz)], pot_hbm.at[f], out_sem.at[f]
                ).start()

    steps = SWEEPS * DEGREE
    end = steps % 2

    @pl.loop(0, steps - 1)
    def _(j):
        step(j, False)

    step(jnp.int32(steps - 1), True)

    for f in range(fields):
        wait_field(end, f)

    def z_copy(p, d, arrives):
        o = d if arrives else d ^ 1
        src = u.at[p, pl.ds(REACH if d == 2 else nz, REACH)]
        dst = u.at[p, pl.ds(0 if o == 2 else nz + REACH, REACH)]
        return pltpu.make_async_remote_copy(
            src_ref=src, dst_ref=dst, send_sem=zsend.at[p, d - 2], recv_sem=zrecv.at[p, o - 2],
            device_id=place[d], device_id_type=MESH,
        )

    def x_copy(p, d, arrives):
        o = d if arrives else d ^ 1
        return pltpu.make_async_remote_copy(
            src_ref=xs.at[p, d], dst_ref=xr.at[p, o], send_sem=xsend.at[p, d],
            recv_sem=xrecv.at[p, o], device_id=place[d], device_id_type=MESH,
        )

    def slope_x(f, z, c):
        return x_up(c, rowx[end, f, 1, z]) - x_down(c, rowx[end, f, 0, z])

    def slope_y(c):
        ahead = jnp.where(lanes == ny - 1, 0.0, pltpu.roll(c, ny - 1, 1))
        return ahead - jnp.where(lanes == 0, 0.0, pltpu.roll(c, 1, 1))

    for p in range(pairs):
        s = pair_ref[p, 0]
        q = pair_ref[p, 1] + 2

        @pl.loop(0, nz, unroll=2)
        def _(z):
            sc = v[end, s, z + 1]
            qc = v[end, q, z + 1]
            total = (v[end, s, z + 2] - v[end, s, z]) * (v[end, q, z + 2] - v[end, q, z])
            total = total + slope_x(s, z, sc) * slope_x(q, z, qc)
            total = total + slope_y(sc) * slope_y(qc)
            raw[z] = (0.25 * cp[z + 1]) * total

        rh, rl = halves(raw[...].reshape(cells, ny))
        smooth = (dot(rl, ty[0]) + dot(rh, ty[1])) + dot(rh, ty[0])
        u[p, REACH:REACH + nz] = smooth.reshape(nz, nx, ny)
        for d in (2, 3):
            @pl.when(has[d])
            def _():
                z_copy(p, d, False).start()

    taps = prior_taps()
    for p in range(pairs):
        for d in (2, 3):
            @pl.when(has[d])
            def _():
                z_copy(p, d, True).wait_recv()

        for z in range(nz):
            total = taps[0] * u[p, z + REACH]
            for k in range(1, REACH + 1):
                total = total + taps[k] * (u[p, z + REACH - k] + u[p, z + REACH + k])
            w[p, z] = total
            xs[p, 0, z * REACH:(z + 1) * REACH] = total[0:REACH]
            xs[p, 1, z * REACH:(z + 1) * REACH] = total[nx - REACH:nx]

        for d in (0, 1):
            @pl.when(has[d])
            def _():
                x_copy(p, d, False).start()

    for p in range(pairs):
        wh, wl = halves(w[p].reshape(cells, ny))
        total = (dot(tc[0], wl) + dot(tc[1], wh)) + dot(tc[0], wh)
        for d in (0, 1):
            @pl.when(has[d])
            def _():
                x_copy(p, d, True).wait_recv()
        for d in (0, 1):
            eh, el = halves(xr[p, d])
            total = total + ((dot(te[d, 0], el) + dot(te[d, 1], eh)) + dot(te[d, 0], eh))
        sens[p] = total.reshape(nz, nx, ny)
        pltpu.make_async_copy(sens.at[p], sens_hbm.at[p], out_sem.at[fields + p]).start()

    for p in range(pairs):
        for d in range(4):
            @pl.when(has[d])
            def _():
                (x_copy if d < 2 else z_copy)(p, d, False).wait_send()
        pltpu.make_async_copy(sens.at[p], sens_hbm.at[p], out_sem.at[fields + p]).wait()
    for f in range(fields):
        pltpu.make_async_copy(
            v.at[end, f, pl.ds(1, nz)], pot_hbm.at[f], out_sem.at[f]
        ).wait()


def local(conductivity, start_fields, electrodes, currents, pair_table, bounds):
    fields, nz, nx, ny = start_fields.shape
    pairs = pair_table.shape[0]
    steps = SWEEPS * DEGREE
    slab = (nz, nx, ny)
    smem = pl.BlockSpec(memory_space=pltpu.SMEM)
    vmem = pl.BlockSpec(memory_space=pltpu.VMEM)
    hbm = pl.BlockSpec(memory_space=pl.ANY)
    rim = nz * REACH
    scratch = [
        pltpu.VMEM((nz + 2, nx, ny), F32),
        pltpu.VMEM((2, fields, nz + 2, nx, ny), F32),
        pltpu.VMEM((fields,) + slab, F32),
        pltpu.VMEM((fields,) + slab, F32),
        pltpu.VMEM((2, fields, 2, nz, 1, ny), F32),
        pltpu.VMEM((fields, 2, nz, 1, ny), F32),
        pltpu.VMEM((2, nz, 1, ny), F32),
        pltpu.VMEM((2, nz, 1, ny), F32),
        pltpu.VMEM((nz + 1, nx, ny), F32),
        pltpu.VMEM(slab, F32),
        pltpu.VMEM(slab, F32),
        pltpu.VMEM(slab, F32),
        pltpu.VMEM(slab, F32),
        pltpu.VMEM(slab, F32),
        pltpu.VMEM(slab, F32),
        pltpu.VMEM((pairs, nz + 2 * REACH, nx, ny), F32),
        pltpu.VMEM((pairs,) + slab, F32),
        pltpu.VMEM((pairs, 2, rim, ny), F32),
        pltpu.VMEM((pairs, 2, rim, ny), F32),
        pltpu.VMEM((pairs,) + slab, F32),
        pltpu.VMEM((steps, 2, 1, ny), F32),
        pltpu.VMEM((2, ny, ny), BF16),
        pltpu.VMEM((2, nz * nx, nz * nx), BF16),
        pltpu.VMEM((2, 2, nz * nx, rim), BF16),
        pltpu.SemaphoreType.DMA((fields + 2,)),
        pltpu.SemaphoreType.DMA((fields + pairs,)),
        pltpu.SemaphoreType.DMA((fields, 4)),
        pltpu.SemaphoreType.DMA((2, fields, 4)),
        pltpu.SemaphoreType.DMA((4,)),
        pltpu.SemaphoreType.DMA((4,)),
        pltpu.SemaphoreType.DMA((pairs, 2)),
        pltpu.SemaphoreType.DMA((pairs, 2)),
        pltpu.SemaphoreType.DMA((pairs, 2)),
        pltpu.SemaphoreType.DMA((pairs, 2)),
    ]
    out = jax.ShapeDtypeStruct((fields,) + slab, F32)
    out_sens = jax.ShapeDtypeStruct((pairs,) + slab, F32)
    return pl.pallas_call(
        kernel,
        out_shape=(out, out_sens),
        in_specs=[smem, smem, vmem, vmem, hbm, hbm],
        out_specs=(hbm, hbm),
        scratch_shapes=scratch,
        compiler_params=pltpu.CompilerParams(
            collective_id=0, has_side_effects=True, vmem_limit_bytes=48 * 1024 * 1024
        ),
    )(pair_table, bounds, electrodes, currents, conductivity, start_fields)


def solution(mesh):
    placed = (P("gz", "xy", None), P(None, "gz", "xy", None), P(), P(), P(), P())
    return jax.shard_map(
        local,
        mesh=mesh,
        in_specs=placed,
        out_specs=(P(None, "gz", "xy", None), P(None, "gz", "xy", None)),
        check_vma=False,
    )
```

profile of v0, /device:TPU:17, one launch (start us, length us, event | category | flops | bytes accessed | tf_op | source)
XLA Modules:
  0.0 87.7 jit_solution(6268548541299649541)
XLA Ops:
  0.6 0.8 copy.8.pair_ref
  1.4 0.0 copy-start
  1.4 1.0 %copy-done = f32[16,16,512]{2,1,0:T(8,128)S(1)} copy-done((f32[16,16,512]{2,1,0:T(8,128)S(1)}, f32[16,16,512]{2,1,0:T(8,128)}, u32[]{:S(2)}) %copy-start) | copy-done | bytes 524312
  2.4 0.0 copy-start.1
  2.4 0.7 copy-done.1
  3.1 0.0 copy-start.2
  3.1 0.7 copy-done.2
  3.8 0.0 copy-start.3
  3.8 0.7 copy-done.3
  4.5 80.6 %shard_map.77 = (f32[4,16,16,512]{3,2,1,0:T(8,128)S(1)}, f32[4,16,16,512]{3,2,1,0:T(8,128)S(1)}) custom-call(s32[4,2]{1,0:T(4,128)S(1)} %copy.8.pair_ref, f32[2]{0:T(128)S(1)} %copy-done.3, s32[3,4,64]{2,1,0:T(4,128)S(1)} %copy-done.1, f32[4,64]{1,0:T(4,128)S(1)} %copy-done.2, f32[16,16,512]{2,1,0:T(8,128)S(1)} %copy-done, f32[4,16,16,512]{3,2,1,0:T(8,128)} %start_hbm.1), custom_call_target="tpu_custom_call" | custom-call | tf_op jit(solution)/shard_map/pallas_call | solution.py:449
  85.1 1.3 %copy.11 = f32[4,16,16,512]{3,2,1,0:T(8,128)} copy(f32[4,16,16,512]{3,2,1,0:T(8,128)S(1)} %get-tuple-element.4) | data formatting | bytes 4194304
  86.4 1.3 %copy.12 = f32[4,16,16,512]{3,2,1,0:T(8,128)} copy(f32[4,16,16,512]{3,2,1,0:T(8,128)S(1)} %get-tuple-element.5) | data formatting | bytes 4194304
Async XLA Ops:
  1.4 1.0 %copy-start = (f32[16,16,512]{2,1,0:T(8,128)S(1)}, f32[16,16,512]{2,1,0:T(8,128)}, u32[]{:S(2)}) copy-start(f32[16,16,512]{2,1,0:T(8,128)} %cond_hbm.1) | copy-start | bytes 1572868
  2.4 0.7 copy-start.1
  3.1 0.7 copy-start.2
  3.8 0.7 copy-start.3
where the time goes:
time: 88 us; the launch traced here: 87.7 us
  Pallas kernels  80.6 us (92%)
  local copies, waits for them, and re-layouts  6.47 us (7%)
    pallas_call x1, Pallas kernels, local(): pl.pallas_call(kernel, out_shape=(out, out_sens), in_specs=[smem, smem, v...  80.6 us
    unnamed x11, local copies, waits for them, and re-layouts  6.47 us

commit v1 on v0

--- a/solution.py
+++ b/solution.py
@@ -244,7 +244,7 @@
             cond_copy(d, True).wait_recv()
             cond_copy(d, False).wait_send()
 
-    @pl.loop(0, nz)
+    @pl.loop(0, nz, unroll=nz)
     def _(z):
         c = cp[z + 1]
         half = 0.5 * c
@@ -272,7 +272,7 @@
         for f in range(fields):
             wait_field(slot, f)
 
-            @pl.loop(0, nz, unroll=2)
+            @pl.loop(0, nz, unroll=nz)
             def _(z):
                 c = v[slot, f, z + 1]
                 total = cz[z] * v[slot, f, z] + cz[z + 1] * v[slot, f, z + 2]
@@ -337,7 +337,7 @@
         s = pair_ref[p, 0]
         q = pair_ref[p, 1] + 2
 
-        @pl.loop(0, nz, unroll=2)
+        @pl.loop(0, nz, unroll=nz)
         def _(z):
             sc = v[end, s, z + 1]
             qc = v[end, q, z + 1]

time: 88 us -> 67.2 us (0.76)
  Pallas kernels: 80.6 us -> 59.9 us
    pallas_call x1, Pallas kernels: 80.6 us -> 59.9 us  [local(): pl.pallas_call(kernel, out_shape=(out, out_sens), in_specs=[smem, smem, v...]
where the time goes in v1:
time: 67.2 us; the launch traced here: 67 us
  Pallas kernels  59.9 us (89%)
  local copies, waits for them, and re-layouts  6.47 us (10%)
    pallas_call x1, Pallas kernels, local(): pl.pallas_call(kernel, out_shape=(out, out_sens), in_specs=[smem, smem, v...  59.9 us
    unnamed x11, local copies, waits for them, and re-layouts  6.47 us

profile of v1, /device:TPU:17, one launch (start us, length us, event | category | flops | bytes accessed | tf_op | source)
XLA Modules:
  0.0 67.0 jit_solution(1818470455188348889)
XLA Ops:
  0.6 0.8 %copy.8.pair_ref = s32[4,2]{1,0:T(4,128)S(1)} copy(s32[4,2]{0,1:T(2,128)} %param.10) | data formatting | bytes 64 | tf_op args[4]
  1.4 0.0 copy-start
  1.4 1.0 %copy-done = f32[16,16,512]{2,1,0:T(8,128)S(1)} copy-done((f32[16,16,512]{2,1,0:T(8,128)S(1)}, f32[16,16,512]{2,1,0:T(8,128)}, u32[]{:S(2)}) %copy-start) | copy-done | bytes 524312
  2.4 0.0 copy-start.1
  2.4 0.7 %copy-done.1 = s32[3,4,64]{2,1,0:T(4,128)S(1)} copy-done((s32[3,4,64]{2,1,0:T(4,128)S(1)}, s32[3,4,64]{2,1,0:T(4,128)}, u32[]{:S(2)}) %copy-start.1) | copy-done | bytes 3096
  3.1 0.0 copy-start.2
  3.1 0.7 %copy-done.2 = f32[4,64]{1,0:T(4,128)S(1)} copy-done((f32[4,64]{1,0:T(4,128)S(1)}, f32[4,64]{1,0:T(4,128)}, u32[]{:S(2)}) %copy-start.2) | copy-done | bytes 1048
  3.8 0.0 copy-start.3
  3.8 0.7 copy-done.3
  4.5 59.9 %shard_map.77 = (f32[4,16,16,512]{3,2,1,0:T(8,128)S(1)}, f32[4,16,16,512]{3,2,1,0:T(8,128)S(1)}) custom-call(s32[4,2]{1,0:T(4,128)S(1)} %copy.8.pair_ref, f32[2]{0:T(128)S(1)} %copy-done.3, s32[3,4,64]{2,1,0:T(4,128)S(1)} %copy-done.1, f32[4,64]{1,0:T(4,128)S(1)} %copy-done.2, f32[16,16,512]{2,1,0:T(8,128)S(1)} %copy-done, f32[4,16,16,512]{3,2,1,0:T(8,128)} %start_hbm.1), custom_call_target="tpu_custom_call" | custom-call | tf_op jit(solution)/shard_map/pallas_call | solution.py:449
  64.3 1.3 %copy.11 = f32[4,16,16,512]{3,2,1,0:T(8,128)} copy(f32[4,16,16,512]{3,2,1,0:T(8,128)S(1)} %get-tuple-element.4) | data formatting | bytes 4194304
  65.7 1.3 %copy.12 = f32[4,16,16,512]{3,2,1,0:T(8,128)} copy(f32[4,16,16,512]{3,2,1,0:T(8,128)S(1)} %get-tuple-element.5) | data formatting | bytes 4194304
Async XLA Ops:
  1.4 1.0 %copy-start = (f32[16,16,512]{2,1,0:T(8,128)S(1)}, f32[16,16,512]{2,1,0:T(8,128)}, u32[]{:S(2)}) copy-start(f32[16,16,512]{2,1,0:T(8,128)} %cond_hbm.1) | copy-start | bytes 1572868
  2.4 0.7 %copy-start.1 = (s32[3,4,64]{2,1,0:T(4,128)S(1)}, s32[3,4,64]{2,1,0:T(4,128)}, u32[]{:S(2)}) copy-start(s32[3,4,64]{2,1,0:T(4,128)} %elec_ref.1) | copy-start | bytes 9220
  3.1 0.7 %copy-start.2 = (f32[4,64]{1,0:T(4,128)S(1)}, f32[4,64]{1,0:T(4,128)}, u32[]{:S(2)}) copy-start(f32[4,64]{1,0:T(4,128)} %cur_ref.1) | copy-start | bytes 3076
  3.8 0.7 copy-start.3

commit v2 on v1

--- a/solution.py
+++ b/solution.py
@@ -56,10 +56,11 @@
 
 
 def kernel(
-    pair_ref, bounds_ref, elec_ref, cur_ref, cond_hbm, start_hbm, pot_hbm, sens_hbm,
+    pair_hbm, bounds_hbm, elec_hbm, cur_hbm, cond_hbm, start_hbm, pot_hbm, sens_hbm,
+    pair_ref, bounds_ref, elec_ref, cur_ref,
     cp, v, x, r, rowx, sfx, rcx, scx, cz, cxm, cxp, cym, cyp, cd, raw, u, w, xs, xr, sens, coef,
     ty, tc, te,
-    load_sem, out_sem, send_sem, recv_sem, csend, crecv, zsend, zrecv, xsend, xrecv,
+    load_sem, small_sem, out_sem, send_sem, recv_sem, csend, crecv, zsend, zrecv, xsend, xrecv,
 ):
     fields, nz, nx, ny = x.shape
     pairs = u.shape[0]
@@ -77,7 +78,14 @@
             pltpu.make_async_copy(start_hbm.at[f], v.at[0, f, pl.ds(1, nz)], load_sem.at[1 + f])
         )
     loads.append(pltpu.make_async_copy(start_hbm, x, load_sem.at[1 + fields]))
-    for copy in loads:
+    small = [
+        pltpu.make_async_copy(src, dst, small_sem.at[i])
+        for i, (src, dst) in enumerate([
+            (pair_hbm, pair_ref), (bounds_hbm, bounds_ref), (elec_hbm, elec_ref),
+            (cur_hbm, cur_ref),
+        ])
+    ]
+    for copy in loads + small:
         copy.start()
 
     for d in range(4):
@@ -174,6 +182,9 @@
             sfx[f, 1, z] = v[0, f, z + 1, nx - 1:nx, :]
 
         send_field(0, f)
+
+    for copy in small:
+        copy.wait()
 
     low = jnp.full((1, ny), bounds_ref[0], F32)
     high = jnp.full((1, ny), bounds_ref[1], F32)
@@ -333,6 +344,48 @@
         ahead = jnp.where(lanes == ny - 1, 0.0, pltpu.roll(c, ny - 1, 1))
         return ahead - jnp.where(lanes == 0, 0.0, pltpu.roll(c, 1, 1))
 
+    def send_depth(p, values):
+        u[p, REACH:REACH + nz] = values
+        for d in (2, 3):
+            @pl.when(has[d])
+            def _():
+                z_copy(p, d, False).start()
+
+    def send_tiles(p):
+        for z in range(nz):
+            values = w[p, z]
+            xs[p, 0, z * REACH:(z + 1) * REACH] = values[0:REACH]
+            xs[p, 1, z * REACH:(z + 1) * REACH] = values[nx - REACH:nx]
+        for d in (0, 1):
+            @pl.when(has[d])
+            def _():
+                x_copy(p, d, False).start()
+
+    taps = prior_taps()
+
+    def smooth_depth(p, out):
+        for d in (2, 3):
+            @pl.when(has[d])
+            def _():
+                z_copy(p, d, True).wait_recv()
+        for z in range(nz):
+            total = taps[0] * u[p, z + REACH]
+            for k in range(1, REACH + 1):
+                total = total + taps[k] * (u[p, z + REACH - k] + u[p, z + REACH + k])
+            out[p, z] = total
+
+    def smooth_tiles(p):
+        wh, wl = halves(w[p].reshape(cells, ny))
+        total = (dot(tc[0], wl) + dot(tc[1], wh)) + dot(tc[0], wh)
+        for d in (0, 1):
+            @pl.when(has[d])
+            def _():
+                x_copy(p, d, True).wait_recv()
+        for d in (0, 1):
+            eh, el = halves(xr[p, d])
+            total = total + ((dot(te[d, 0], el) + dot(te[d, 1], eh)) + dot(te[d, 0], eh))
+        return total.reshape(nz, nx, ny)
+
     for p in range(pairs):
         s = pair_ref[p, 0]
         q = pair_ref[p, 1] + 2
@@ -348,43 +401,23 @@
 
         rh, rl = halves(raw[...].reshape(cells, ny))
         smooth = (dot(rl, ty[0]) + dot(rh, ty[1])) + dot(rh, ty[0])
-        u[p, REACH:REACH + nz] = smooth.reshape(nz, nx, ny)
-        for d in (2, 3):
-            @pl.when(has[d])
-            def _():
-                z_copy(p, d, False).start()
-
-    taps = prior_taps()
+        if p % 2 == 0:
+            send_depth(p, smooth.reshape(nz, nx, ny))
+        else:
+            w[p] = smooth.reshape(nz, nx, ny)
+            send_tiles(p)
+
     for p in range(pairs):
-        for d in (2, 3):
-            @pl.when(has[d])
-            def _():
-                z_copy(p, d, True).wait_recv()
-
-        for z in range(nz):
-            total = taps[0] * u[p, z + REACH]
-            for k in range(1, REACH + 1):
-                total = total + taps[k] * (u[p, z + REACH - k] + u[p, z + REACH + k])
-            w[p, z] = total
-            xs[p, 0, z * REACH:(z + 1) * REACH] = total[0:REACH]
-            xs[p, 1, z * REACH:(z + 1) * REACH] = total[nx - REACH:nx]
-
-        for d in (0, 1):
-            @pl.when(has[d])
-            def _():
-                x_copy(p, d, False).start()
-
+        if p % 2 == 0:
+            smooth_depth(p, w)
+            send_tiles(p)
+        else:
+            send_depth(p, smooth_tiles(p))
     for p in range(pairs):
-        wh, wl = halves(w[p].reshape(cells, ny))
-        total = (dot(tc[0], wl) + dot(tc[1], wh)) + dot(tc[0], wh)
-        for d in (0, 1):
-            @pl.when(has[d])
-            def _():
-                x_copy(p, d, True).wait_recv()
-        for d in (0, 1):
-            eh, el = halves(xr[p, d])
-            total = total + ((dot(te[d, 0], el) + dot(te[d, 1], eh)) + dot(te[d, 0], eh))
-        sens[p] = total.reshape(nz, nx, ny)
+        if p % 2 == 0:
+            sens[p] = smooth_tiles(p)
+        else:
+            smooth_depth(p, sens)
         pltpu.make_async_copy(sens.at[p], sens_hbm.at[p], out_sem.at[fields + p]).start()
 
     for p in range(pairs):
@@ -404,11 +437,13 @@
     pairs = pair_table.shape[0]
     steps = SWEEPS * DEGREE
     slab = (nz, nx, ny)
-    smem = pl.BlockSpec(memory_space=pltpu.SMEM)
-    vmem = pl.BlockSpec(memory_space=pltpu.VMEM)
     hbm = pl.BlockSpec(memory_space=pl.ANY)
     rim = nz * REACH
     scratch = [
+        pltpu.SMEM(pair_table.shape, jnp.int32),
+        pltpu.SMEM(bounds.shape, F32),
+        pltpu.VMEM(electrodes.shape, jnp.int32),
+        pltpu.VMEM(currents.shape, F32),
         pltpu.VMEM((nz + 2, nx, ny), F32),
         pltpu.VMEM((2, fields, nz + 2, nx, ny), F32),
         pltpu.VMEM((fields,) + slab, F32),
@@ -434,6 +469,7 @@
         pltpu.VMEM((2, nz * nx, nz * nx), BF16),
         pltpu.VMEM((2, 2, nz * nx, rim), BF16),
         pltpu.SemaphoreType.DMA((fields + 2,)),
+        pltpu.SemaphoreType.DMA((4,)),
         pltpu.SemaphoreType.DMA((fields + pairs,)),
         pltpu.SemaphoreType.DMA((fields, 4)),
         pltpu.SemaphoreType.DMA((2, fields, 4)),
@@ -449,7 +485,7 @@
     return pl.pallas_call(
         kernel,
         out_shape=(out, out_sens),
-        in_specs=[smem, smem, vmem, vmem, hbm, hbm],
+        in_specs=[hbm] * 6,
         out_specs=(hbm, hbm),
         scratch_shapes=scratch,
         compiler_params=pltpu.CompilerParams(

time: 67.2 us -> 63.5 us (0.945)
  Pallas kernels: 59.9 us -> 56 us
    pallas_call x1, Pallas kernels: 59.9 us -> 56 us  [local(): pl.pallas_call(kernel, out_shape=(out, out_sens), in_specs=[hbm] * 6, out...]
where the time goes in v2:
time: 63.5 us; the launch traced here: 63.1 us
  Pallas kernels  56 us (88%)
  local copies, waits for them, and re-layouts  6.47 us (10%)
  between operations  0.64 us (1%)
    pallas_call x1, Pallas kernels, local(): pl.pallas_call(kernel, out_shape=(out, out_sens), in_specs=[hbm] * 6, out...  56 us
    unnamed x11, local copies, waits for them, and re-layouts  6.47 us

profile of v2, /device:TPU:17, one launch (start us, length us, event | category | flops | bytes accessed | tf_op | source)
XLA Modules:
  0.0 63.1 jit_solution(13688001296369793095)
XLA Ops:
  0.6 0.8 %copy.8.pair_hbm = s32[4,2]{1,0:T(4,128)S(1)} copy(s32[4,2]{0,1:T(2,128)} %param.10) | data formatting | bytes 64 | tf_op args[4]
  1.4 0.0 copy-start
  1.4 1.0 %copy-done = f32[16,16,512]{2,1,0:T(8,128)S(1)} copy-done((f32[16,16,512]{2,1,0:T(8,128)S(1)}, f32[16,16,512]{2,1,0:T(8,128)}, u32[]{:S(2)}) %copy-start) | copy-done | bytes 524312
  2.4 0.0 copy-start.1
  2.4 0.7 %copy-done.1 = s32[3,4,64]{2,1,0:T(4,128)S(1)} copy-done((s32[3,4,64]{2,1,0:T(4,128)S(1)}, s32[3,4,64]{2,1,0:T(4,128)}, u32[]{:S(2)}) %copy-start.1) | copy-done | bytes 3096
  3.1 0.0 copy-start.2
  3.1 0.7 %copy-done.2 = f32[4,64]{1,0:T(4,128)S(1)} copy-done((f32[4,64]{1,0:T(4,128)S(1)}, f32[4,64]{1,0:T(4,128)}, u32[]{:S(2)}) %copy-start.2) | copy-done | bytes 1048
  3.8 0.0 copy-start.3
  3.8 0.7 %copy-done.3 = f32[2]{0:T(128)S(1)} copy-done((f32[2]{0:T(128)S(1)}, f32[2]{0:T(128)}, u32[]{:S(2)}) %copy-start.3) | copy-done | bytes 32
  4.5 56.0 %shard_map.77 = (f32[4,16,16,512]{3,2,1,0:T(8,128)S(1)}, f32[4,16,16,512]{3,2,1,0:T(8,128)S(1)}) custom-call(s32[4,2]{1,0:T(4,128)S(1)} %copy.8.pair_hbm, f32[2]{0:T(128)S(1)} %copy-done.3, s32[3,4,64]{2,1,0:T(4,128)S(1)} %copy-done.1, f32[4,64]{1,0:T(4,128)S(1)} %copy-done.2, f32[16,16,512]{2,1,0:T(8,128)S(1)} %copy-done, f32[4,16,16,512]{3,2,1,0:T(8,128)} %start_hbm.1), custom_call_target="tpu_custom_call" | custom-call | tf_op jit(solution)/shard_map/pallas_call | solution.py:485
  60.5 1.3 %copy.11 = f32[4,16,16,512]{3,2,1,0:T(8,128)} copy(f32[4,16,16,512]{3,2,1,0:T(8,128)S(1)} %get-tuple-element.4) | data formatting | bytes 4194304
  61.8 1.3 %copy.12 = f32[4,16,16,512]{3,2,1,0:T(8,128)} copy(f32[4,16,16,512]{3,2,1,0:T(8,128)S(1)} %get-tuple-element.5) | data formatting | bytes 4194304
Async XLA Ops:
  1.4 1.0 %copy-start = (f32[16,16,512]{2,1,0:T(8,128)S(1)}, f32[16,16,512]{2,1,0:T(8,128)}, u32[]{:S(2)}) copy-start(f32[16,16,512]{2,1,0:T(8,128)} %cond_hbm.1) | copy-start | bytes 1572868
  2.4 0.7 %copy-start.1 = (s32[3,4,64]{2,1,0:T(4,128)S(1)}, s32[3,4,64]{2,1,0:T(4,128)}, u32[]{:S(2)}) copy-start(s32[3,4,64]{2,1,0:T(4,128)} %elec_hbm.1) | copy-start | bytes 9220
  3.1 0.7 %copy-start.2 = (f32[4,64]{1,0:T(4,128)S(1)}, f32[4,64]{1,0:T(4,128)}, u32[]{:S(2)}) copy-start(f32[4,64]{1,0:T(4,128)} %cur_hbm.1) | copy-start | bytes 3076
  3.8 0.7 %copy-start.3 = (f32[2]{0:T(128)S(1)}, f32[2]{0:T(128)}, u32[]{:S(2)}) copy-start(f32[2]{0:T(128)} %bounds_hbm.1) | copy-start | bytes 28

commit v3 on v2

--- a/solution.py
+++ b/solution.py
@@ -489,7 +489,7 @@
         out_specs=(hbm, hbm),
         scratch_shapes=scratch,
         compiler_params=pltpu.CompilerParams(
-            collective_id=0, has_side_effects=True, vmem_limit_bytes=48 * 1024 * 1024
+            collective_id=0, has_side_effects=True, vmem_limit_bytes=62 * 1024 * 1024
         ),
     )(pair_table, bounds, electrodes, currents, conductivity, start_fields)
 

time: 63.5 us -> 64 us (level)
  Pallas kernels: 56 us -> 56.8 us
    pallas_call x1, Pallas kernels: 56 us -> 56.8 us  [local(): pl.pallas_call(kernel, out_shape=(out, out_sens), in_specs=[hbm] * 6, out...]
    unnamed x11 -> x5, local copies, waits for them, and re-layouts: 6.47 us -> 6.03 us
where the time goes in v3:
time: 64 us; the launch traced here: 63.5 us
  Pallas kernels  56.8 us (89%)
  local copies, waits for them, and re-layouts  6.03 us (9%)
  between operations  0.65 us (1%)
    pallas_call x1, Pallas kernels, local(): pl.pallas_call(kernel, out_shape=(out, out_sens), in_specs=[hbm] * 6, out...  56.8 us
    unnamed x5, local copies, waits for them, and re-layouts  6.03 us

profile of v3, /device:TPU:17, one launch (start us, length us, event | category | flops | bytes accessed | tf_op | source)
XLA Modules:
  0.0 63.5 jit_solution(6983115462723619632)
XLA Ops:
  0.6 1.3 %copy.8.pair_hbm = s32[4,2]{1,0:T(4,128)} copy(s32[4,2]{0,1:T(2,128)} %param.10) | data formatting | bytes 64 | tf_op args[4]
  2.0 56.8 %shard_map.77 = (f32[4,16,16,512]{3,2,1,0:T(8,128)}, f32[4,16,16,512]{3,2,1,0:T(8,128)}) custom-call(s32[4,2]{1,0:T(4,128)} %copy.8.pair_hbm, f32[2]{0:T(128)} %bounds_hbm.1, s32[3,4,64]{2,1,0:T(4,128)} %elec_hbm.1, f32[4,64]{1,0:T(4,128)} %cur_hbm.1, f32[16,16,512]{2,1,0:T(8,128)} %cond_hbm.1, f32[4,16,16,512]{3,2,1,0:T(8,128)} %start_hbm.1), custom_call_target="tpu_custom_call" | custom-call | tf_op jit(solution)/shard_map/pallas_call | solution.py:485
  58.8 0.0 copy-start
  58.8 3.4 %copy.11 = f32[4,16,16,512]{3,2,1,0:T(8,128)} copy(f32[4,16,16,512]{3,2,1,0:T(8,128)} %get-tuple-element.4) | data formatting | bytes 4194304
  62.1 0.0 copy-done
  62.2 1.3 %copy.12 = f32[4,16,16,512]{3,2,1,0:T(8,128)} copy(f32[4,16,16,512]{3,2,1,0:T(8,128)S(1)} %copy-done) | data formatting | bytes 4194304
Async XLA Ops:
  58.8 3.4 %copy-start = (f32[4,16,16,512]{3,2,1,0:T(8,128)S(1)}, f32[4,16,16,512]{3,2,1,0:T(8,128)}, u32[]{:S(2)}) copy-start(f32[4,16,16,512]{3,2,1,0:T(8,128)} %get-tuple-element.5) | copy-start | bytes 6291460
